TPU v7x, 256 devices: a whole 4x4x8 slice. The times are simulated.
256 devices in a mesh: ctx: 32 (over x, y, core), head: 8 (over z).
Axes of the slice: x: 4, y: 4, z: 8, core: 2. Of those that a mesh axis runs over, the one named last changes fastest.
Arguments:
- query: bfloat16 [512, 64, 128], P('ctx', 'head'), may hold values from -6 to 6
- weights: bfloat16 [512, 64], P('ctx', 'head'), as said below
- keys: bfloat16 [65536, 128], P('ctx'), may hold values from -6 to 6
- main_logits: bfloat16 [512, 65536], P(None, 'ctx'), as said below
- row_weight: float32 [512], replicated, may hold values from 4 to 40
- offset: int32 [1], replicated, may hold values from 64512 to 65024
Outputs:
- query_grad: float32 [512, 64, 128], P('ctx', 'head')
- key_grad: float32 [65536, 128], P(('ctx', 'head'))
- weight_grad: float32 [512, 64], P('ctx', 'head')
Inputs may be any that keep to these rules, and one draw needn't show every extreme that they name: query row t of the block sits at position offset + t. Finite weights. `main_logits`: finite logits.
All inputs are finite; a program needn't handle non-finite values.
Results may differ from a plain program's by a relative error of at most 0.0065.
Values may be sent and summed in bfloat16 or wider, within the bound.
A program may use at most 64 MiB of HBM per device.

v0:
```python
import jax
import jax.numpy as jnp
from jax import lax
from jax.sharding import PartitionSpec as P

masked_value = -1e30


def exp_total(masked, peak, allowed):
    return jnp.sum(jnp.where(allowed, jnp.exp(masked - peak[:, None]), 0.0), axis=1)


def global_stats(masked, tmasked, allowed):
    peak = jnp.max(masked, axis=1)
    tpeak = jnp.max(tmasked, axis=1)
    peak, tpeak = lax.pmax((peak, tpeak), ("ctx", "head"))
    total, ttotal = lax.psum(
        (exp_total(masked, peak, allowed), exp_total(tmasked, tpeak, allowed)), ("ctx", "head")
    )
    return (peak, total, tpeak, ttotal)


def finish_grad(masked, tmasked, allowed, stats, row_weight, loss_scale):
    peak, total, tpeak, ttotal = stats
    index_prob = jnp.where(allowed, jnp.exp(masked - peak[:, None]), 0.0) / total[:, None]
    target = jnp.where(allowed, jnp.exp(tmasked - tpeak[:, None]), 0.0) / ttotal[:, None]
    return jnp.where(allowed, row_weight[:, None] * loss_scale * (index_prob - target), 0.0).astype(
        jnp.bfloat16
    )


def per_device(query, weights, keys, main_logits, row_weight, offset):
    gathered_q, gathered_w = (
        lax.all_gather(query, "ctx", axis=0, tiled=True),
        lax.all_gather(weights, "ctx", axis=0, tiled=True),
    )
    rows_total = gathered_q.shape[0]
    heads_here = gathered_q.shape[1]
    depth = gathered_q.shape[2]
    key_count = keys.shape[0]
    block_len = min(512, key_count)
    nblocks = key_count // block_len
    total_keys = key_count * lax.axis_size("ctx")
    head_scale = depth ** (-0.5)
    loss_scale = float(total_keys) ** 0.5
    high = lax.Precision.HIGHEST
    weight_f = gathered_w.astype(jnp.float32)
    key_blocks = keys.reshape(nblocks, block_len, depth)

    def forward_block(key_block):
        dotted = jnp.einsum(
            "thd,sd->ths", gathered_q, key_block, preferred_element_type=jnp.float32
        )
        active = jnp.maximum(dotted, 0.0) * head_scale
        return jnp.einsum("th,ths->ts", weight_f, active, precision=high)

    partial_scores = jnp.moveaxis(lax.map(forward_block, key_blocks), 0, 1).reshape(
        rows_total, key_count
    )
    limit = offset[0] + jnp.arange(rows_total, dtype=jnp.int32)[:, None]
    ctx_first = lax.axis_index("ctx") * key_count
    share_width = key_count // lax.axis_size("head")
    share_first = lax.axis_index("head") * share_width
    scores = lax.psum(partial_scores, "head")
    positions = ctx_first + jnp.arange(key_count, dtype=jnp.int32)
    allowed = positions[None, :] <= limit
    masked = jnp.where(allowed, scores, masked_value)
    tmasked = jnp.where(allowed, main_logits.astype(jnp.float32), masked_value)
    share_masked = lax.dynamic_slice_in_dim(masked, share_first, share_width, 1)
    share_tmasked = lax.dynamic_slice_in_dim(tmasked, share_first, share_width, 1)
    share_allowed = lax.dynamic_slice_in_dim(allowed, share_first, share_width, 1)
    stats = global_stats(share_masked, share_tmasked, share_allowed)
    score_grad = finish_grad(masked, tmasked, allowed, stats, row_weight, loss_scale)
    grad_blocks = jnp.moveaxis(score_grad.reshape(rows_total, nblocks, block_len), 1, 0)

    def backward_block(carry, inputs):
        query_acc, weight_acc = carry
        key_block, grad_block = inputs
        dotted = jnp.einsum(
            "thd,sd->ths", gathered_q, key_block, preferred_element_type=jnp.float32
        )
        active = jnp.maximum(dotted, 0.0) * head_scale
        grad_f = grad_block.astype(jnp.float32)
        pre_grad = jnp.where(
            dotted > 0, grad_f[:, None, :] * weight_f[:, :, None] * head_scale, 0.0
        ).astype(jnp.bfloat16)
        query_acc = query_acc + jnp.einsum(
            "ths,sd->thd", pre_grad, key_block, preferred_element_type=jnp.float32
        )
        weight_acc = weight_acc + jnp.einsum("ts,ths->th", grad_f, active, precision=high)
        key_part = jnp.einsum(
            "ths,thd->sd", pre_grad, gathered_q, preferred_element_type=jnp.float32
        )
        return ((query_acc, weight_acc), key_part)

    start_carry = (
        jnp.zeros((rows_total, heads_here, depth), jnp.float32),
        jnp.zeros((rows_total, heads_here), jnp.float32),
    )
    (query_acc, weight_acc), key_parts = lax.scan(
        backward_block, start_carry, (key_blocks, grad_blocks)
    )
    key_grad = lax.psum_scatter(
        key_parts.reshape(key_count, depth), "head", scatter_dimension=0, tiled=True
    )
    query_grad, weight_grad = (
        lax.psum_scatter(query_acc, "ctx", scatter_dimension=0, tiled=True),
        lax.psum_scatter(weight_acc, "ctx", scatter_dimension=0, tiled=True),
    )
    return (query_grad, key_grad, weight_grad)


def solution(mesh):
    in_specs = (P("ctx", "head", None), P("ctx", "head"), P("ctx", None), P(None, "ctx"), P(), P())
    out_specs = (P("ctx", "head", None), P(("ctx", "head"), None), P("ctx", "head"))
    return jax.shard_map(
        per_device, mesh=mesh, in_specs=in_specs, out_specs=out_specs, check_vma=False
    )
```

profile of v0, /device:TPU:1, one launch (start us, length us, event | category | flops | bytes accessed | tf_op | source)
XLA Modules:
  0.0 629.8 jit_solution(2943701992925834892)
XLA Ops:
  7.2 1.4 copy.28
  8.7 25.8 %all-gather = bf16[32,16,8]{1,2,0:T(8,128)(2,1)S(1)} all-gather(bf16[1,16,8]{1,2,0:T(8,128)(2,1)} %bitcast.82), channel_id=1, replica_groups=mesh['ctx'=32,'head'=8] {'ctx'}, dimensions={0}, use_global_device_ids=true | all-gather | bytes 8448 | tf_op jit(solution)/shard_map/all_gather | solution.py:35
  34.8 28.5 %all-gather.3.cloned.1.call-done = bf16[512,8,128]{2,0,1:T(8,128)(2,1)} async-done(((bf16[16,8,128]{2,0,1:T(8,128)(2,1)}), bf16[512,8,128]{2,0,1:T(8,128)(2,1)}) %all-gather.3.cloned.1.call-update) | async-done | bytes 1048592 | tf_op jit(solution)/shard_map/all_gather | solution.py:34
  63.3 17.9 %while.25 = (s32[]{:T(128)}, f32[4,512,512]{1,2,0:T(8,128)}, bf16[4,512,128]{2,1,0:T(8,128)(2,1)}, bf16[512,8,128]{2,0,1:T(8,128)(2,1)}, f32[512,8]{0,1:T(8,128)S(1)}, /*index=5*/s32[]{:T(128)}) while((s32[]{:T(128)}, f32[4,512,512]{1,2,0:T(8,128)}, bf16[4,512,128]{2,1,0:T(8,128)(2,1)}, bf16[512,8,128]{2,0,1:T(8,128)(2,1)}, ...), condition=%wide.region_1.2_spmd, body=%wide.region_0.1_spmd.sunk | while | flops 544997376 | bytes 8537157 | solution.py:57
  63.3 2.7 fusion.31
  66.7 1.0 constant_dynamic-update-slice_fusion.2
  67.7 2.7 fusion.31
  71.1 1.1 constant_dynamic-update-slice_fusion.2
  72.2 2.7 fusion.31
  75.6 1.1 constant_dynamic-update-slice_fusion.2
  76.7 2.7 fusion.31
  80.1 1.0 constant_dynamic-update-slice_fusion.2
  81.9 2.9 copy.32
  85.6 103.7 %all-reduce.4.cloned.1.call-done = f32[512,2048]{0,1:T(8,128)} async-done(((f32[512,2048]{0,1:T(8,128)}), f32[512,2048]{0,1:T(8,128)}) %all-reduce.4.cloned.1.call-update) | async-done | bytes 4194320 | tf_op jit(solution)/shard_map/psum | solution.py:64
  189.4 2.7 compare_select_fusion.2
  192.0 2.0 copy-done.2
  194.1 1.2 copy-done.3
  195.3 76.4 %all-reduce.1 = (f32[512]{0:T(512)S(1)}, f32[512]{0:T(512)S(1)}) all-reduce(f32[512]{0:T(512)S(1)} %get-tuple-element.152, f32[512]{0:T(512)S(1)} %get-tuple-element.151), channel_id=1, replica_groups=mesh['ctx'=32,'head'=8] {'ctx','head'}, use_global_device_ids=true, to_apply=%region_4.5 | all-reduce | flops 1024 | bytes 8192 | tf_op jit(solution)/shard_map/pmax | solution.py:16
  271.7 1.4 select_reduce_fusion.1
  273.1 72.2 %all-reduce = (f32[512]{0:T(512)S(1)}, f32[512]{0:T(512)S(1)}) all-reduce(f32[512]{0:T(512)S(1)} %get-tuple-element.116, f32[512]{0:T(512)S(1)} %get-tuple-element.115), channel_id=1, replica_groups=mesh['ctx'=32,'head'=8] {'ctx','head'}, use_global_device_ids=true, to_apply=%region_10.11 | all-reduce | flops 1024 | bytes 8192 | tf_op jit(solution)/shard_map/psum | solution.py:17
  345.4 5.2 fusion.17
  350.6 61.7 %while.26 = (s32[]{:T(128)}, f32[512,8,128]{2,0,1:T(8,128)}, f32[512,8]{0,1:T(8,128)S(1)}, f32[4,512,128]{2,1,0:T(8,128)}, bf16[4,512,128]{2,1,0:T(8,128)(2,1)},...) while((s32[]{:T(128)}, f32[512,8,128]{2,0,1:T(8,128)}, ...), condition=%wide.region_12.13_spmd.clone, body=%wide.region_11.12_spmd.clone.sunk | while | flops 1641287680 | bytes 70354568 | solution.py:100
  350.6 1.2 bitcast_convert_fusion.2
  351.8 2.2 fusion.35
  354.0 3.2 copy-done
  357.2 2.0 fusion.36
  359.2 6.4 %select_add_fusion.4 = f32[512,8,128]{2,0,1:T(8,128)} fusion(f32[512,8,128]{2,0,1:T(8,128)} %get-tuple-element.266, pred[]{:T(512)S(6)} %compare.3, bf16[4,512,128]{2,1,0:T(8,128)(2,1)} %get-tuple-element.279, s32[]{:T(128)} %get-tuple-element.265, f32[512,512,8]{1,0,2:T(8,128)} %copy-done, f32[512,8]{0,1:T(8,128)S(1)} %get-tuple-element.282, ...), kind=kOutput, calls=%fused_computation.9.clone.1 | convolution fusion | flops 548405248 | bytes 13779457 | tf_op jit(solution)/shard_map/while/body/eval_jaxpr/ths,sd->thd/dot_general | solution.py:87
  365.6 1.2 bitcast_convert_fusion.2
  366.7 2.2 fusion.35
  368.9 3.2 copy-done
  372.2 2.0 fusion.36
  374.1 7.0 %select_add_fusion.4 = f32[512,8,128]{2,0,1:T(8,128)} fusion(f32[512,8,128]{2,0,1:T(8,128)} %get-tuple-element.266, pred[]{:T(512)S(6)} %compare.3, bf16[4,512,128]{2,1,0:T(8,128)(2,1)} %get-tuple-element.279, s32[]{:T(128)} %get-tuple-element.265, f32[512,512,8]{1,0,2:T(8,128)} %copy-done, f32[512,8]{0,1:T(8,128)S(1)} %get-tuple-element.282, ...), kind=kOutput, calls=%fused_computation.9.clone.1 | convolution fusion | flops 548405248 | bytes 13779457 | tf_op jit(solution)/shard_map/while/body/eval_jaxpr/ths,sd->thd/dot_general | solution.py:87
  381.1 1.2 bitcast_convert_fusion.2
  382.3 2.2 fusion.35
  384.5 3.2 copy-done
  387.7 2.0 fusion.36
  389.7 7.0 %select_add_fusion.4 = f32[512,8,128]{2,0,1:T(8,128)} fusion(f32[512,8,128]{2,0,1:T(8,128)} %get-tuple-element.266, pred[]{:T(512)S(6)} %compare.3, bf16[4,512,128]{2,1,0:T(8,128)(2,1)} %get-tuple-element.279, s32[]{:T(128)} %get-tuple-element.265, f32[512,512,8]{1,0,2:T(8,128)} %copy-done, f32[512,8]{0,1:T(8,128)S(1)} %get-tuple-element.282, ...), kind=kOutput, calls=%fused_computation.9.clone.1 | convolution fusion | flops 548405248 | bytes 13779457 | tf_op jit(solution)/shard_map/while/body/eval_jaxpr/ths,sd->thd/dot_general | solution.py:87
  396.7 1.2 bitcast_convert_fusion.2
  397.9 2.2 fusion.35
  400.1 3.2 copy-done
  403.3 2.0 fusion.36
  405.3 7.0 %select_add_fusion.4 = f32[512,8,128]{2,0,1:T(8,128)} fusion(f32[512,8,128]{2,0,1:T(8,128)} %get-tuple-element.266, pred[]{:T(512)S(6)} %compare.3, bf16[4,512,128]{2,1,0:T(8,128)(2,1)} %get-tuple-element.279, s32[]{:T(128)} %get-tuple-element.265, f32[512,512,8]{1,0,2:T(8,128)} %copy-done, f32[512,8]{0,1:T(8,128)S(1)} %get-tuple-element.282, ...), kind=kOutput, calls=%fused_computation.9.clone.1 | convolution fusion | flops 548405248 | bytes 13779457 | tf_op jit(solution)/shard_map/while/body/eval_jaxpr/ths,sd->thd/dot_general | solution.py:87
  412.3 0.8 copy.45
  413.8 4.2 copy.33
  418.0 74.5 %reduce-scatter.10.cloned.1.call-done = f32[16,8]{1,0:T(8,128)} async-done(((f32[512,8]{1,0:T(8,128)}), f32[16,8]{1,0:T(8,128)}) %reduce-scatter.10.cloned.1.call-update) | async-done | bytes 528
  492.5 1.4 copy.46
  493.9 36.8 %reduce-scatter.8.cloned.1.call-done = f32[256,128]{1,0:T(8,128)} async-done(((f32[2048,128]{1,0:T(8,128)}), f32[256,128]{1,0:T(8,128)}) %reduce-scatter.8.cloned.1.call-update) | async-done | bytes 131088 | tf_op jit(solution)/shard_map/reduce_scatter | solution.py:103
  530.6 92.7 %reduce-scatter.6.cloned.1.call-done = f32[16,8,128]{2,1,0:T(8,128)} async-done(((f32[512,8,128]{2,1,0:T(8,128)}), f32[16,8,128]{2,1,0:T(8,128)}) %reduce-scatter.6.cloned.1.call-update) | async-done | bytes 65552 | tf_op jit(solution)/shard_map/reduce_scatter | solution.py:107
  (44 shorter events, 4.7 us)
Async XLA Ops:
  7.2 56.1 %all-gather.3.cloned.1.call-start = ((), (), s32[]{:S(2)}) async-start(), calls=%async_computation.3 | async-start | bytes 1081344 | tf_op jit(solution)/shard_map/all_gather | solution.py:34
  8.6 180.7 %all-reduce.4.cloned.1.call-start = ((), (), s32[]{:S(2)}) async-start(), calls=%async_computation.4 | async-start | bytes 8388608 | tf_op jit(solution)/shard_map/psum | solution.py:64
  81.2 3.7 copy-start.4
  81.2 411.3 %reduce-scatter.10.cloned.1.call-start = ((), (), s32[]{:S(2)}) async-start(), calls=%async_computation.7 | async-start | bytes 270336
  192.0 2.0 copy-start.2
  192.0 3.2 copy-start.3
  345.4 5.2 copy-start.1
  354.0 3.2 copy-start
  368.9 3.2 copy-start
  384.5 3.2 copy-start
  400.1 3.2 copy-start
  413.2 117.5 %reduce-scatter.8.cloned.1.call-start = ((), (), s32[]{:S(2)}) async-start(), calls=%async_computation.6 | async-start | bytes 1179648 | tf_op jit(solution)/shard_map/reduce_scatter | solution.py:103
  413.7 209.5 %reduce-scatter.6.cloned.1.call-start = ((), (), s32[]{:S(2)}) async-start(), calls=%async_computation.5 | async-start | bytes 2162688 | tf_op jit(solution)/shard_map/reduce_scatter | solution.py:107
Sparse Core Ops, SparseCore 0:
  11.0 52.1 all-gather.2
  81.3 107.9 all-reduce.3
  413.3 79.1 reduce-scatter.9
  495.5 35.1 reduce-scatter.7
  534.9 88.3 reduce-scatter.5
where the time goes:
time: 631 us; the launch traced here: 630 us
  waiting for transfers between devices  337 us (53%)
  blocking collectives  174 us (28%)
  matrix products  55 us (9%)
  local copies, waits for them, and re-layouts  33.9 us (5%)
  other arithmetic  14.8 us (2%)
  between operations  14.6 us (2%)
    psum x1, waiting for transfers between devices, per_device(): scores = lax.psum(partial_scores, 'head')  104 us
    reduce_scatter x1, waiting for transfers between devices, per_device(): lax.psum_scatter(query_acc, 'ctx', scatter_dimension=0, tiled=True)  92.7 us
    pmax x1, blocking collectives, global_stats(): peak, tpeak = lax.pmax((peak, tpeak), ('ctx', 'head'))  76.4 us
    unnamed x6, waiting for transfers between devices  75.1 us
    psum x1, blocking collectives, global_stats(): lax.psum((exp_total(masked, peak, allowed), exp_total(tmasked, tpeak, all...  72.2 us
    reduce_scatter x1, waiting for transfers between devices, per_device(): lax.psum_scatter(key_parts.reshape(key_count, depth), 'head', scatter_dim...  36.8 us
    all_gather x1, waiting for transfers between devices, per_device(): lax.all_gather(query, 'ctx', axis=0, tiled=True)  28.5 us
    dot_general x4, matrix products, backward_block(): jnp.einsum('ths,sd->thd', pre_grad, key_block, preferred_element_type=jnp...  27.3 us
  transfers between devices with their start and end apart: 5, of which 5 were waited for; matrix products, arithmetic and copies ran while one was open for 2% of the time, Pallas kernels for 0%

commit v1 on v0

v1 whole, which is shorter than its diff:
```python
import functools

import jax
import jax.numpy as jnp
from jax import lax
from jax.experimental import pallas as pl
from jax.experimental.pallas import tpu as pltpu
from jax.sharding import PartitionSpec as P

MESH = pl.DeviceIdType.MESH
masked_value = -1e30
bf16 = jnp.bfloat16
f32 = jnp.float32

NX, NY, NZ = 4, 4, 8
CHIPS = NX * NY
SLOTS = 2 * CHIPS
ROWS = 64
KEYS = 2048
DH = 128
BLOCK = 128
GROUP = 4
CHUNK = 256
NCHUNK = KEYS // CHUNK


def iota(shape, dim):
    return lax.broadcasted_iota(jnp.int32, shape, dim)


def fold_rows(tiles):
    sub = iota(tiles[0].shape, 0)
    for k in (4, 2, 1):
        low = (sub & k) == 0
        half = len(tiles) // 2
        out = []
        for a, b in zip(tiles[:half], tiles[half:]):
            out.append(
                jnp.where(low, a + pltpu.roll(a, 8 - k, 0), b + pltpu.roll(b, k, 0))
            )
        tiles = out
    return tiles[0]


def kernel(
    query,
    weights,
    keys_hbm,
    logits_hbm,
    row_weight,
    offset,
    query_grad,
    key_grad,
    weight_grad,
    keys,
    keys_t,
    logits,
    send_a,
    recv_a,
    slots,
    relu,
    score,
    target,
    grad_rows,
    query_w,
    row_scale,
    stat_own,
    stat_in,
    sib_out,
    sib_in,
    sum_out,
    sum_in,
    ring_out,
    ring_in,
    back_out,
    back_in,
    local_sem,
    a_send,
    a_recv,
    g_send,
    g_recv,
    s_send,
    s_recv,
    st_send,
    st_recv,
    sib_send,
    sib_recv,
    sum_send,
    sum_recv,
    ring_send,
    ring_recv,
    back_send,
    back_recv,
):
    ctx = lax.axis_index("ctx")
    z = lax.axis_index("head")
    core = ctx % 2
    chip = ctx // 2
    x = chip // NY
    y = chip % NY
    head_scale = DH**-0.5
    loss_scale = float(KEYS * 32) ** 0.5

    def chip_at(dx, dy):
        return ((x + dx) % NX) * NY + (y + dy) % NY

    def dev_chip(dx, dy):
        return {"ctx": chip_at(dx, dy) * 2 + core, "head": z}

    def dev_z(dz):
        return {"ctx": ctx, "head": (z + dz) % NZ}

    sibling = {"ctx": chip * 2 + (1 - core), "head": z}

    def send(src, dst, send_sem, recv_sem, device):
        copy = pltpu.make_async_remote_copy(
            src_ref=src,
            dst_ref=dst,
            send_sem=send_sem,
            recv_sem=recv_sem,
            device_id=device,
            device_id_type=MESH,
        )
        copy.start()
        return copy

    load_keys = pltpu.make_async_copy(keys_hbm, keys, local_sem.at[0])
    load_keys.start()
    load_logits = pltpu.make_async_copy(logits_hbm, logits, local_sem.at[1])
    load_logits.start()
    barrier = pltpu.get_barrier_semaphore()

    def greet(i, carry):
        pl.semaphore_signal(
            barrier, inc=1, device_id=dev_chip(i // NY, i % NY), device_id_type=MESH
        )
        return carry

    lax.fori_loop(1, CHIPS, greet, 0)

    def greet_z(i, carry):
        pl.semaphore_signal(barrier, inc=1, device_id=dev_z(i), device_id_type=MESH)
        return carry

    lax.fori_loop(1, NZ, greet_z, 0)
    pl.semaphore_signal(barrier, inc=1, device_id=sibling, device_id_type=MESH)

    w_own = weights[...].astype(f32)
    lane = iota((8, 128), 1)
    place = jnp.where(
        (lane % 8 == iota((8, 128), 0)) & ((lane % 64) // 8 == z), 1.0, 0.0
    ).astype(f32)
    w_spread = jnp.dot(w_own, place, preferred_element_type=f32)
    pair = iota((16, 128), 0) % 2 == iota((16, 128), 1) // 64
    w_spread = jnp.where(pair, w_spread, 0.0)
    for to in range(NZ):
        send_a[to, 0:16, :] = query[16 * to : 16 * to + 16, :]
        row = w_spread[2 * to : 2 * to + 1, :] + w_spread[2 * to + 1 : 2 * to + 2, :]
        send_a[to, 16:32, :] = jnp.broadcast_to(row, (16, 128)).astype(bf16)

    def row_of(shape):
        r = iota(shape, 0)
        slot = (r // 8) * 4 + r % 4
        return 16 * ((slot % CHIPS) * 2 + slot // CHIPS) + 2 * z + (r // 4) % 2

    here = row_of((ROWS, 512)) == iota((ROWS, 512), 1)
    rw_col = jnp.sum(jnp.where(here, row_weight[...], 0.0), axis=1, keepdims=True)
    row_scale[...] = jnp.broadcast_to(rw_col * loss_scale, (ROWS, 128))

    load_keys.wait()
    for i in range(KEYS // 256):
        keys_t[:, 256 * i : 256 * i + 256] = (
            keys[256 * i : 256 * i + 256, :].astype(f32).T.astype(bf16)
        )
    load_logits.wait()
    pick = jnp.where(here, 1.0, 0.0).astype(bf16)
    limit = offset[0] - ctx * KEYS
    allowed = iota((ROWS, KEYS), 1) <= limit + row_of((ROWS, KEYS))
    tmasked = jnp.where(
        allowed, jnp.dot(pick, logits[...], preferred_element_type=f32), masked_value
    )
    tpeak = jnp.max(tmasked, axis=1, keepdims=True)
    texp = jnp.where(allowed, jnp.exp(tmasked - tpeak), 0.0)
    target[...] = texp
    ttotal = jnp.sum(texp, axis=1, keepdims=True)

    pl.semaphore_wait(barrier, CHIPS - 1 + NZ - 1 + 1)

    def start_a(i, carry):
        to = (z + i) % NZ
        send(send_a.at[to], recv_a.at[z], a_send.at[i], a_recv.at[i], dev_z(i))
        return carry

    lax.fori_loop(1, NZ, start_a, 0)
    recv_a[pl.ds(z, 1)] = send_a[pl.ds(z, 1)]

    def wait_a(i, carry):
        pltpu.make_async_remote_copy(
            src_ref=send_a.at[(z + i) % NZ],
            dst_ref=recv_a.at[(z + NZ - i) % NZ],
            send_sem=a_send.at[i],
            recv_sem=a_recv.at[i],
            device_id=dev_z(i),
            device_id_type=MESH,
        ).wait()
        return carry

    lax.fori_loop(1, NZ, wait_a, 0)
    own_slot = core * CHIPS + chip
    got = recv_a[...].astype(f32)
    mine = got[:, 0:16, :].reshape(8, 2, 8, DH)
    own = jnp.concatenate([mine[:, 0].reshape(64, DH), mine[:, 1].reshape(64, DH)], axis=0)
    own_w = jnp.sum(got[:, 16:32, :], axis=0)
    slots[pl.ds(own_slot, 1), 0:BLOCK, :] = own.astype(bf16)[None]
    slots[pl.ds(own_slot, 1), BLOCK : BLOCK + 16, :] = own_w.astype(bf16)[None]

    def start_g(i, carry):
        send(
            slots.at[own_slot],
            slots.at[own_slot],
            g_send.at[i],
            g_recv.at[i],
            dev_chip(i // NY, i % NY),
        )
        return carry

    lax.fori_loop(1, CHIPS, start_g, 0)

    def relay(i, carry):
        slot = core * CHIPS + chip_at(NX - i // NY, NY - i % NY)

        @pl.when(i > 0)
        def _():
            pltpu.make_async_remote_copy(
                src_ref=slots.at[own_slot],
                dst_ref=slots.at[slot],
                send_sem=g_send.at[i],
                recv_sem=g_recv.at[i],
                device_id=dev_chip(i // NY, i % NY),
                device_id_type=MESH,
            ).wait()

        send(slots.at[slot], slots.at[slot], s_send.at[i], s_recv.at[i], sibling)
        return carry

    lax.fori_loop(0, CHIPS, relay, 0)

    def wait_relay(i, carry):
        p = chip_at(NX - i // NY, NY - i % NY)
        pltpu.make_async_remote_copy(
            src_ref=slots.at[core * CHIPS + p],
            dst_ref=slots.at[(1 - core) * CHIPS + p],
            send_sem=s_send.at[i],
            recv_sem=s_recv.at[i],
            device_id=sibling,
            device_id_type=MESH,
        ).wait()
        return carry

    lax.fori_loop(0, CHIPS, wait_relay, 0)

    def forward(gi, carry):
        block = slots[pl.ds(gi * GROUP, GROUP)]
        q = block[:, 0:BLOCK, :].reshape(GROUP * BLOCK, DH)
        w_tiles = []
        for i in range(GROUP):
            w_row = block[i, BLOCK : BLOCK + 16, :].astype(f32)[0:1] * head_scale
            w_col = jnp.broadcast_to(w_row, (128, 128)).T
            w_tiles.append(w_col.reshape(2, 8, 8, 128))
            qw = block[i, 0:BLOCK, :].astype(f32) * w_col
            query_w[:, pl.ds(pl.multiple_of((gi * GROUP + i) * 128, 128), 128)] = qw.T.astype(bf16)
        for c in range(NCHUNK):
            at = slice(c * CHUNK, (c + 1) * CHUNK)
            dotted = jnp.dot(q, keys_t[:, at], preferred_element_type=f32)
            active = jnp.maximum(dotted, 0.0)
            relu[pl.ds(gi * GROUP, GROUP), :, at] = active.reshape(GROUP, BLOCK, CHUNK).astype(bf16)
            active = active.reshape(GROUP, 2, 8, 8, CHUNK)
            for l in range(CHUNK // 128):
                tiles = []
                for j in range(2):
                    for i in range(GROUP):
                        part = active[i, j, :, :, l * 128 : l * 128 + 128] * w_tiles[i][j]
                        tiles.append(jnp.sum(part, axis=0))
                score[
                    pl.ds(pl.multiple_of(gi * 8, 8), 8),
                    c * CHUNK + l * 128 : c * CHUNK + l * 128 + 128,
                ] = fold_rows(tiles)
        return carry

    lax.fori_loop(0, SLOTS // GROUP, forward, 0)

    masked = jnp.where(allowed, score[...], masked_value)
    peak = jnp.max(masked, axis=1, keepdims=True)
    exps = jnp.where(allowed, jnp.exp(masked - peak), 0.0)
    score[...] = exps
    total = jnp.sum(exps, axis=1, keepdims=True)
    lane = iota((ROWS, 128), 1)
    stats = jnp.where(
        lane == 0,
        peak,
        jnp.where(lane == 1, total, jnp.where(lane == 2, tpeak, jnp.where(lane == 3, ttotal, 0.0))),
    )
    stats = jnp.concatenate([stats, jnp.zeros((128 - ROWS, 128), f32)], axis=0).T[0:8]
    local_stats = stats

    def merge(parts):
        rows = []
        for k in (0, 2):
            top = functools.reduce(jnp.maximum, [p[k : k + 1] for p in parts])
            rows.append(top)
            rows.append(sum(p[k + 1 : k + 2] * jnp.exp(p[k : k + 1] - top) for p in parts))
        return jnp.concatenate(rows + [jnp.zeros((4, 128), f32)], axis=0)

    at = 0
    for stage, peers in enumerate(
        (
            [sibling],
            [dev_chip(0, d) for d in (1, 2, 3)],
            [dev_chip(d, 0) for d in (1, 2, 3)],
        )
    ):
        stat_own[stage] = stats
        copies = []
        for n, peer in enumerate(peers):
            copies.append(
                send(
                    stat_own.at[stage],
                    stat_in.at[at + n],
                    st_send.at[at + n],
                    st_recv.at[at + n],
                    peer,
                )
            )
        for copy in copies:
            copy.wait()
        stats = merge([stats] + [stat_in[at + n] for n in range(len(peers))])
        at += len(peers)

    shares = [
        jnp.exp(local_stats[k : k + 1] - stats[k : k + 1]) / stats[k + 1 : k + 2] for k in (0, 2)
    ]
    shares = jnp.concatenate(shares + [jnp.zeros((126, 128), f32)], axis=0).T[0:ROWS]
    prob_scale = shares[:, 0:1] * row_scale[:, 0:1]
    target_scale = shares[:, 1:2] * row_scale[:, 0:1]
    score[...] = score[...] * prob_scale - target[...] * target_scale

    def backward_query(gi):
        tile = score[pl.ds(pl.multiple_of(gi * 8, 8), 8), :]
        acc = jnp.zeros((GROUP * BLOCK, DH), f32)
        for c in range(NCHUNK):
            at = slice(c * CHUNK, (c + 1) * CHUNK)
            parts = []
            for i in range(GROUP):
                for j in range(2):
                    row = tile[j * 4 + i : j * 4 + i + 1, at]
                    row = jnp.broadcast_to(row, (16, CHUNK)).astype(bf16)
                    grad_rows[gi * GROUP + i, j, :, at] = row
                    act = relu[gi * GROUP + i, j * 64 : j * 64 + 64, at].reshape(4, 16, CHUNK)
                    parts.append(jnp.where(act > 0, row[None], jnp.zeros_like(act)).reshape(64, CHUNK))
            pre = jnp.concatenate(parts, axis=0)
            acc = acc + jnp.dot(pre, keys[at, :], preferred_element_type=f32)
        return acc.reshape(GROUP, BLOCK, DH)

    def for_sibling(g, carry):
        acc = backward_query((1 - core) * (CHIPS // GROUP) + g)
        sib_out[pl.ds(g * GROUP, GROUP)] = acc.astype(bf16)
        send(
            sib_out.at[pl.ds(g * GROUP, GROUP)],
            sib_in.at[pl.ds(g * GROUP, GROUP)],
            sib_send.at[g],
            sib_recv.at[g],
            sibling,
        )
        return carry

    lax.fori_loop(0, CHIPS // GROUP, for_sibling, 0)

    def for_chips(n, carry):
        dx = (n + 2) % NX
        g = (x + dx) % NX
        acc = backward_query(core * (CHIPS // GROUP) + g)
        pltpu.make_async_remote_copy(
            src_ref=sib_out.at[pl.ds(g * GROUP, GROUP)],
            dst_ref=sib_in.at[pl.ds(g * GROUP, GROUP)],
            send_sem=sib_send.at[g],
            recv_sem=sib_recv.at[g],
            device_id=sibling,
            device_id_type=MESH,
        ).wait()
        acc = acc + sib_in[pl.ds(g * GROUP, GROUP)].astype(f32)
        sum_out[pl.ds(g * GROUP, GROUP)] = acc.astype(bf16)

        def to_chip(dy, c2):
            i = dx * NY + dy

            @pl.when(i > 0)
            def _():
                send(
                    sum_out.at[chip_at(dx, dy)],
                    sum_in.at[i],
                    sum_send.at[i],
                    sum_recv.at[i],
                    dev_chip(dx, dy),
                )

            return c2

        lax.fori_loop(0, NY, to_chip, 0)
        return carry

    lax.fori_loop(0, NX, for_chips, 0)

    def key_chunk(dz):
        at = pl.ds(pl.multiple_of(((z + dz) % NZ) * CHUNK, CHUNK), CHUNK)
        act = relu[:, :, at].reshape(SLOTS, 2, 4, 16, CHUNK)
        rows = grad_rows[:, :, :, at].reshape(SLOTS, 2, 1, 16, CHUNK)
        pre = jnp.where(act > 0, rows, jnp.zeros_like(rows)).reshape(SLOTS * BLOCK, CHUNK)
        return jnp.dot(query_w[...], pre, preferred_element_type=f32)

    half = DH // 2
    part = key_chunk(4).astype(bf16)
    ring_out[0] = part
    up = send(
        ring_out.at[0, pl.ds(0, half)],
        ring_in.at[0, pl.ds(0, half)],
        ring_send.at[0],
        ring_recv.at[0],
        dev_z(1),
    )
    down = send(
        ring_out.at[0, pl.ds(half, half)],
        ring_in.at[0, pl.ds(half, half)],
        ring_send.at[1],
        ring_recv.at[1],
        dev_z(NZ - 1),
    )
    for n in (1, 2, 3):
        ahead = key_chunk(4 - n)
        up.wait()
        if n == 1:
            got = ring_in[0, 0:half, :].astype(f32)
            ahead = ahead + jnp.concatenate([got, jnp.zeros((half, CHUNK), f32)], axis=0)
        else:
            ahead = ahead + ring_in[2 * n - 3].astype(f32)
        ring_out[2 * n - 1] = ahead.astype(bf16)
        up = send(
            ring_out.at[2 * n - 1],
            ring_in.at[2 * n - 1],
            ring_send.at[2 * n],
            ring_recv.at[2 * n],
            dev_z(1),
        )
        behind = key_chunk(4 + n)
        down.wait()
        if n == 1:
            got = ring_in[0, half:DH, :].astype(f32)
            behind = behind + jnp.concatenate([jnp.zeros((half, CHUNK), f32), got], axis=0)
        else:
            behind = behind + ring_in[2 * n - 2].astype(f32)
        ring_out[2 * n] = behind.astype(bf16)
        down = send(
            ring_out.at[2 * n],
            ring_in.at[2 * n],
            ring_send.at[2 * n + 1],
            ring_recv.at[2 * n + 1],
            dev_z(NZ - 1),
        )
    own_part = key_chunk(0)

    total_g = sum_out[chip].astype(f32)
    def wait_sum(i, acc):
        pltpu.make_async_remote_copy(
            src_ref=sum_out.at[chip_at(i // NY, i % NY)],
            dst_ref=sum_in.at[i],
            send_sem=sum_send.at[i],
            recv_sem=sum_recv.at[i],
            device_id=dev_chip(i // NY, i % NY),
            device_id_type=MESH,
        ).wait()
        return acc + sum_in[i].astype(f32)

    total_g = lax.fori_loop(1, CHIPS, wait_sum, total_g)
    total_g = total_g.reshape(2, 8, 8, DH)
    for h in range(NZ):
        back_out[h, 0:8, :] = total_g[0, h]
        back_out[h, 8:16, :] = total_g[1, h]

    def start_back(i, carry):
        send(back_out.at[(z + i) % NZ], back_in.at[z], back_send.at[i], back_recv.at[i], dev_z(i))
        return carry

    lax.fori_loop(1, NZ, start_back, 0)
    back_in[pl.ds(z, 1)] = back_out[pl.ds(z, 1)]

    up.wait()
    down.wait()
    key_sum = own_part + ring_in[5].astype(f32) + ring_in[6].astype(f32)
    key_grad[...] = key_sum.T

    def wait_back(i, carry):
        pltpu.make_async_remote_copy(
            src_ref=back_out.at[(z + i) % NZ],
            dst_ref=back_in.at[(z + NZ - i) % NZ],
            send_sem=back_send.at[i],
            recv_sem=back_recv.at[i],
            device_id=dev_z(i),
            device_id_type=MESH,
        ).wait()
        return carry

    lax.fori_loop(1, NZ, wait_back, 0)
    grad = back_in[...].reshape(128, DH)
    spread = jnp.where(iota((128, 16), 0) // 8 == iota((128, 16), 1), 1.0, 0.0)
    w_rows = jnp.dot(spread, w_own, preferred_element_type=f32)
    w_rows = jnp.where(iota((128, 8), 0) % 8 == iota((128, 8), 1), w_rows, 0.0)
    w_col = jnp.sum(w_rows, axis=1, keepdims=True)
    query_grad[...] = grad * (w_col * head_scale)
    w_grad = jnp.sum(grad * query[...].astype(f32), axis=1, keepdims=True) * head_scale
    w_grad = jnp.where(iota((128, 128), 0) % 8 == iota((128, 128), 1), w_grad, 0.0)
    weight_grad[...] = jnp.sum(w_grad.reshape(16, 8, 128), axis=1)[:, 0:8]


def per_device(query, weights, keys, main_logits, row_weight, offset):
    vmem = pl.BlockSpec(memory_space=pltpu.VMEM)
    anywhere = pl.BlockSpec(memory_space=pl.ANY)
    dma = pltpu.SemaphoreType.DMA
    query_grad, key_grad, weight_grad = pl.pallas_call(
        kernel,
        out_shape=[
            jax.ShapeDtypeStruct((128, DH), f32),
            jax.ShapeDtypeStruct((CHUNK, DH), f32),
            jax.ShapeDtypeStruct((16, 8), f32),
        ],
        in_specs=[
            vmem,
            vmem,
            anywhere,
            anywhere,
            vmem,
            pl.BlockSpec(memory_space=pltpu.SMEM),
        ],
        out_specs=[vmem, vmem, vmem],
        scratch_shapes=[
            pltpu.VMEM((KEYS, DH), bf16),
            pltpu.VMEM((DH, KEYS), bf16),
            pltpu.VMEM((512, KEYS), bf16),
            pltpu.VMEM((NZ, 32, 128), bf16),
            pltpu.VMEM((NZ, 32, 128), bf16),
            pltpu.VMEM((SLOTS, BLOCK + 16, DH), bf16),
            pltpu.VMEM((SLOTS, BLOCK, KEYS), bf16),
            pltpu.VMEM((ROWS, KEYS), f32),
            pltpu.VMEM((ROWS, KEYS), f32),
            pltpu.VMEM((SLOTS, 2, 16, KEYS), bf16),
            pltpu.VMEM((DH, SLOTS * BLOCK), bf16),
            pltpu.VMEM((ROWS, 128), f32),
            pltpu.VMEM((3, 8, 128), f32),
            pltpu.VMEM((7, 8, 128), f32),
            pltpu.VMEM((CHIPS, BLOCK, DH), bf16),
            pltpu.VMEM((CHIPS, BLOCK, DH), bf16),
            pltpu.VMEM((CHIPS, BLOCK, DH), bf16),
            pltpu.VMEM((CHIPS, BLOCK, DH), bf16),
            pltpu.VMEM((7, DH, CHUNK), bf16),
            pltpu.VMEM((7, DH, CHUNK), bf16),
            pltpu.VMEM((NZ, 16, DH), f32),
            pltpu.VMEM((NZ, 16, DH), f32),
            dma((2,)),
            dma((NZ,)),
            dma((NZ,)),
            dma((CHIPS,)),
            dma((CHIPS,)),
            dma((CHIPS,)),
            dma((CHIPS,)),
            dma((7,)),
            dma((7,)),
            dma((CHIPS // GROUP,)),
            dma((CHIPS // GROUP,)),
            dma((CHIPS,)),
            dma((CHIPS,)),
            dma((8,)),
            dma((8,)),
            dma((NZ,)),
            dma((NZ,)),
        ],
        compiler_params=pltpu.CompilerParams(
            collective_id=0, has_side_effects=True, vmem_limit_bytes=56 * 2**20
        ),
    )(
        query.reshape(128, DH),
        weights,
        keys,
        main_logits,
        row_weight.reshape(1, 512),
        offset,
    )
    return query_grad.reshape(16, 8, DH), key_grad, weight_grad


def solution(mesh):
    in_specs = (P("ctx", "head", None), P("ctx", "head"), P("ctx", None), P(None, "ctx"), P(), P())
    out_specs = (P("ctx", "head", None), P(("ctx", "head"), None), P("ctx", "head"))
    return jax.shard_map(
        per_device, mesh=mesh, in_specs=in_specs, out_specs=out_specs, check_vma=False
    )
```

time: 631 us -> 74 us (0.12)
  the two profiles are of different devices: /device:TPU:1 before, /device:TPU:8 now
where the time goes in v1:
time: 74 us; the launch traced here: 73.7 us
  Pallas kernels  66.7 us (90%)
  local copies, waits for them, and re-layouts  5.74 us (8%)
  between operations  1.29 us (2%)
    pallas_call x1, Pallas kernels, per_device(): pl.pallas_call(kernel, out_shape=[jax.ShapeDtypeStruct((128, DH), f32), j...  66.7 us
    unnamed x4, local copies, waits for them, and re-layouts  5.74 us

profile of v1, /device:TPU:8, one launch (start us, length us, event | category | flops | bytes accessed | tf_op | source)
XLA Modules:
  0.0 73.7 jit_solution(5270230234781825189)
XLA Ops:
  1.3 1.3 %copy.9.weights = bf16[16,8]{1,0:T(8,128)(2,1)} copy(bf16[16,8]{0,1:T(8,128)(2,1)} %param.7) | data formatting | bytes 512 | tf_op args[1]
  2.6 66.7 %shard_map.85 = (f32[128,128]{1,0:T(8,128)}, f32[256,128]{1,0:T(8,128)}, f32[16,8]{1,0:T(8,128)}) custom-call(bf16[128,128]{1,0:T(8,128)(2,1)} %bitcast.4, bf16[16,8]{1,0:T(8,128)(2,1)} %copy.9.weights, bf16[2048,128]{1,0:T(8,128)(2,1)} %keys_hbm.1, bf16[512,2048]{1,0:T(8,128)(2,1)} %logits_hbm.1, f32[1,512]{1,0:T(1,128)} %bitcast.5, s32[1]{0:T(128)S(6)} %copy.13.offset), custom_call_target="tpu_custom_call" | custom-call | tf_op jit(solution)/shard_map/pallas_call | solution.py:527
  69.3 1.4 %copy.10 = f32[16,8]{0,1:T(8,128)} copy(f32[16,8]{1,0:T(8,128)} %get-tuple-element.11) | data formatting | bytes 1024
  70.6 1.5 %copy.14 = f32[16,8,128]{2,1,0:T(8,128)} copy(f32[16,8,128]{2,1,0:T(8,128)} %bitcast.3) | data formatting | bytes 131072
  72.1 1.6 %copy.15 = f32[256,128]{1,0:T(8,128)} copy(f32[256,128]{1,0:T(8,128)} %get-tuple-element.16) | data formatting | bytes 262144

commit v2 on v0

v2 whole, which is shorter than its diff:
```python
import functools

import jax
import jax.numpy as jnp
from jax import lax
from jax.experimental import pallas as pl
from jax.experimental.pallas import tpu as pltpu
from jax.sharding import PartitionSpec as P

MESH = pl.DeviceIdType.MESH
masked_value = -1e30
bf16 = jnp.bfloat16
f32 = jnp.float32

NX, NY, NZ = 4, 4, 8
CHIPS = NX * NY
ROWS = 2 * CHIPS
KEYS = 2048
BOTH = 2 * KEYS
DH = 128
BLOCK = 128
GROUP = 4
CHUNK = 256
NCHUNK = BOTH // CHUNK


def iota(shape, dim):
    return lax.broadcasted_iota(jnp.int32, shape, dim)


def fold_rows(tiles):
    sub = iota(tiles[0].shape, 0)
    for k in (4, 2, 1):
        low = (sub & k) == 0
        half = len(tiles) // 2
        out = []
        for a, b in zip(tiles[:half], tiles[half:]):
            out.append(
                jnp.where(low, a + pltpu.roll(a, 8 - k, 0), b + pltpu.roll(b, k, 0))
            )
        tiles = out
    return tiles[0]


def copy_of(src, dst, send_sem, recv_sem, device):
    return pltpu.make_async_remote_copy(
        src_ref=src,
        dst_ref=dst,
        send_sem=send_sem,
        recv_sem=recv_sem,
        device_id=device,
        device_id_type=MESH,
    )


def kernel(
    query_hbm,
    weights_hbm,
    keys_hbm,
    logits_hbm,
    row_weight,
    offset,
    back,
    key_sum,
    query,
    weights,
    keys,
    keys_t,
    logits,
    own_logits,
    sib_logits,
    send_a,
    recv_a,
    slots,
    relu,
    score,
    target,
    grad_rows,
    query_w,
    row_scale,
    stat_in,
    sum_out,
    sum_in,
    key_own,
    key_sib_out,
    key_sib_in,
    key_out,
    key_in,
    back_out,
    back_in,
    local_sem,
    a_send,
    a_recv,
    k_send,
    k_recv,
    g_send,
    g_recv,
    st_send,
    st_recv,
    sum_send,
    sum_recv,
    sib_send,
    sib_recv,
    key_send,
    key_recv,
    back_send,
    back_recv,
):
    ctx = lax.axis_index("ctx")
    z = lax.axis_index("head")
    core = ctx % 2
    chip = ctx // 2
    x = chip // NY
    y = chip % NY
    head_scale = DH**-0.5
    loss_scale = float(KEYS * 2 * CHIPS) ** 0.5

    def chip_at(dx, dy):
        return ((x + dx) % NX) * NY + (y + dy) % NY

    def dev_chip(dx, dy):
        return {"ctx": chip_at(dx, dy) * 2 + core, "head": z}

    def dev_z(dz):
        return {"ctx": ctx, "head": (z + dz) % NZ}

    sibling = {"ctx": chip * 2 + (1 - core), "head": z}

    load_query = pltpu.make_async_copy(query_hbm, query, local_sem.at[0])
    load_query.start()
    load_weights = pltpu.make_async_copy(weights_hbm, weights, local_sem.at[1])
    load_weights.start()
    own_keys = keys.at[pl.ds(core * KEYS, KEYS)]
    load_keys = pltpu.make_async_copy(keys_hbm, own_keys, local_sem.at[2])
    load_keys.start()
    load_logits = pltpu.make_async_copy(logits_hbm, logits, local_sem.at[3])
    load_logits.start()
    barrier = pltpu.get_barrier_semaphore()

    def greet_z(i, carry):
        pl.semaphore_signal(barrier, inc=1, device_id=dev_z(i), device_id_type=MESH)
        return carry

    lax.fori_loop(1, NZ, greet_z, 0)

    def greet(i, carry):
        pl.semaphore_signal(
            barrier, inc=1, device_id=dev_chip(i // NY, i % NY), device_id_type=MESH
        )
        return carry

    lax.fori_loop(1, CHIPS, greet, 0)
    pl.semaphore_signal(barrier, inc=1, device_id=sibling, device_id_type=MESH)

    lane = iota((8, 128), 1)
    place = jnp.where(
        (lane % 8 == iota((8, 128), 0)) & ((lane % 64) // 8 == z), 1.0, 0.0
    ).astype(f32)
    pair = iota((16, 128), 0) % 2 == iota((16, 128), 1) // 64
    load_weights.wait()
    w_spread = lax.dot_general(
        weights[...].astype(f32), place, (((0,), (0,)), ((), ())), preferred_element_type=f32
    )
    w_spread = jnp.where(pair, w_spread, 0.0)
    load_query.wait()
    for to in range(NZ):
        send_a[to, 0:16, :] = query[16 * to : 16 * to + 16, :]
        row = w_spread[2 * to : 2 * to + 1, :] + w_spread[2 * to + 1 : 2 * to + 2, :]
        send_a[to, 16:32, :] = jnp.broadcast_to(row, (16, 128)).astype(bf16)
    pl.semaphore_wait(barrier, CHIPS - 1 + NZ - 1 + 1)

    def a_copy(i):
        return copy_of(
            send_a.at[(z + i) % NZ], recv_a.at[z], a_send.at[i], a_recv.at[i], dev_z(i)
        )

    def start_a(i, carry):
        a_copy(i).start()
        return carry

    lax.fori_loop(1, NZ, start_a, 0)
    recv_a[pl.ds(z, 1)] = send_a[pl.ds(z, 1)]

    load_keys.wait()
    share_keys = copy_of(own_keys, own_keys, k_send.at[0], k_recv.at[0], sibling)
    share_keys.start()

    def transpose_keys(first):
        for i in range(KEYS // 256):
            at = pl.ds(pl.multiple_of(first * KEYS + 256 * i, 256), 256)
            keys_t[:, at] = keys[at, :].astype(f32).T.astype(bf16)

    transpose_keys(core)

    def wait_a(i, carry):
        copy_of(
            send_a.at[(z + i) % NZ],
            recv_a.at[(z + NZ - i) % NZ],
            a_send.at[i],
            a_recv.at[i],
            dev_z(i),
        ).wait()
        return carry

    lax.fori_loop(1, NZ, wait_a, 0)
    got = recv_a[...].astype(f32)
    mine = got[:, 0:16, :].reshape(8, 2, 8, DH)
    own = jnp.concatenate([mine[:, 0].reshape(64, DH), mine[:, 1].reshape(64, DH)], axis=0)
    own_w = jnp.sum(got[:, 16:32, :], axis=0)
    slots[pl.ds(chip, 1), 0:BLOCK, :] = own.astype(bf16)[None]
    slots[pl.ds(chip, 1), BLOCK : BLOCK + 16, :] = own_w.astype(bf16)[None]

    def near_first(n):
        return n + (n // 2) * (1 - 2 * (n % 2))

    def start_g(m, carry):
        dx = near_first(m // NY)
        dy = near_first(m % NY)
        i = dx * NY + dy
        copy_of(
            slots.at[chip], slots.at[chip], g_send.at[i], g_recv.at[i], dev_chip(dx, dy)
        ).start()
        return carry

    lax.fori_loop(1, CHIPS, start_g, 0)

    def row_of(shape, of_core):
        r = iota(shape, 0)
        slot = (r // 8) * 4 + r % 4
        return 16 * (slot * 2 + of_core) + 2 * z + (r // 4) % 2

    here = row_of((ROWS, 512), core) == iota((ROWS, 512), 1)
    there = row_of((ROWS, 512), 1 - core) == iota((ROWS, 512), 1)
    rw_col = jnp.sum(jnp.where(here, row_weight[...], 0.0), axis=1, keepdims=True)
    row_scale[...] = jnp.broadcast_to(rw_col * loss_scale, (ROWS, 128))
    load_logits.wait()
    pick = jnp.where(there, 1.0, 0.0).astype(bf16)
    sib_logits[...] = jnp.dot(pick, logits[...], preferred_element_type=f32).astype(bf16)
    share_logits = copy_of(
        sib_logits, own_logits.at[core], k_send.at[1], k_recv.at[1], sibling
    )
    share_logits.start()
    pick = jnp.where(here, 1.0, 0.0).astype(bf16)
    own_logits[pl.ds(core, 1)] = jnp.dot(
        pick, logits[...], preferred_element_type=f32
    ).astype(bf16)[None]
    share_keys.wait()
    transpose_keys(1 - core)
    limit = offset[0] - chip * BOTH

    def is_allowed():
        return iota((ROWS, BOTH), 1) <= limit + row_of((ROWS, BOTH), core)

    share_logits.wait()
    tlogits = jnp.concatenate([own_logits[0], own_logits[1]], axis=1).astype(f32)
    tmasked = jnp.where(is_allowed(), tlogits, masked_value)
    tpeak = jnp.max(tmasked, axis=1, keepdims=True)
    texp = jnp.where(is_allowed(), jnp.exp(tmasked - tpeak), 0.0)
    target[...] = texp
    ttotal = jnp.sum(texp, axis=1, keepdims=True)

    def forward(m, carry):
        dx = near_first(m)
        gi = (x + NX - dx) % NX

        def arrive(dy, c2):
            i = dx * NY + dy

            @pl.when(i > 0)
            def _():
                copy_of(
                    slots.at[chip],
                    slots.at[chip_at(NX - dx, NY - dy)],
                    g_send.at[i],
                    g_recv.at[i],
                    dev_chip(dx, dy),
                ).wait()

            return c2

        lax.fori_loop(0, NY, arrive, 0)
        block = slots[pl.ds(gi * GROUP, GROUP)]
        q = block[:, 0:BLOCK, :].reshape(GROUP * BLOCK, DH)
        w_tiles = []
        for i in range(GROUP):
            w_row = block[i, BLOCK : BLOCK + 16, :].astype(f32)[0:1] * head_scale
            w_col = jnp.broadcast_to(w_row, (128, 128)).T
            w_tiles.append(w_col.reshape(2, 8, 8, 128))
            qw = block[i, 0:BLOCK, :].astype(f32) * w_col
            query_w[:, pl.ds(pl.multiple_of((gi * GROUP + i) * 128, 128), 128)] = qw.T.astype(bf16)
        for c in range(NCHUNK):
            at = slice(c * CHUNK, (c + 1) * CHUNK)
            dotted = jnp.dot(q, keys_t[:, at], preferred_element_type=f32)
            active = jnp.maximum(dotted, 0.0)
            relu[pl.ds(gi * GROUP, GROUP), :, at] = active.reshape(GROUP, BLOCK, CHUNK).astype(bf16)
            active = active.reshape(GROUP, 2, 8, 8, CHUNK)
            for l in range(CHUNK // 128):
                tiles = []
                for j in range(2):
                    for i in range(GROUP):
                        part = active[i, j, :, :, l * 128 : l * 128 + 128] * w_tiles[i][j]
                        tiles.append(jnp.sum(part, axis=0))
                score[
                    pl.ds(pl.multiple_of(gi * 8, 8), 8),
                    c * CHUNK + l * 128 : c * CHUNK + l * 128 + 128,
                ] = fold_rows(tiles)
        return carry

    lax.fori_loop(0, NX, forward, 0)

    masked = jnp.where(is_allowed(), score[...], masked_value)
    peak = jnp.max(masked, axis=1, keepdims=True)
    exps = jnp.where(is_allowed(), jnp.exp(masked - peak), 0.0)
    score[...] = exps
    total = jnp.sum(exps, axis=1, keepdims=True)
    lane = iota((ROWS, 128), 1)
    stats = jnp.where(
        lane == 0,
        peak,
        jnp.where(lane == 1, total, jnp.where(lane == 2, tpeak, jnp.where(lane == 3, ttotal, 0.0))),
    )
    local = jnp.concatenate([stats, jnp.zeros((128 - ROWS, 128), f32)], axis=0).T[0:8]
    stat_in[0] = local

    def stat_copy(i):
        return copy_of(
            stat_in.at[0], stat_in.at[i], st_send.at[i], st_recv.at[i], dev_chip(i // NY, i % NY)
        )

    def start_stat(i, carry):
        stat_copy(i).start()
        return carry

    lax.fori_loop(1, CHIPS, start_stat, 0)

    def wait_stat(i, carry):
        stat_copy(i).wait()
        return carry

    lax.fori_loop(1, CHIPS, wait_stat, 0)
    every = [stat_in[i] for i in range(CHIPS)]
    top = functools.reduce(jnp.maximum, every)
    total = sum(s * pltpu.roll(jnp.exp(s - top), 1, 0) for s in every)
    total = jnp.where(iota((8, 128), 0) < 4, total, 1.0)
    shares = jnp.exp(local - top) / pltpu.roll(total, 7, 0)
    shares = jnp.concatenate([shares, jnp.zeros((120, 128), f32)], axis=0).T[0:ROWS]
    prob_scale = shares[:, 0:1] * row_scale[:, 0:1]
    target_scale = shares[:, 2:3] * row_scale[:, 0:1]
    score[...] = score[...] * prob_scale - target[...] * target_scale
    for i in range(NX):
        for j in range(2):
            for k in range(GROUP):
                row = score[i * 8 + j * 4 + k : i * 8 + j * 4 + k + 1, :]
                grad_rows[i * GROUP + k, j] = jnp.broadcast_to(row, (16, BOTH)).astype(bf16)

    def key_place(n):
        return (1 - n % 2) * (4 + n // 2) + (n % 2) * ((7 - n) // 2)

    def key_chunk(of_core, dz):
        first = of_core * KEYS + ((z + dz) % NZ) * CHUNK
        at = pl.ds(pl.multiple_of(first, CHUNK), CHUNK)
        act = relu[:, :, at].reshape(CHIPS, 2, 4, 16, CHUNK)
        rows = grad_rows[:, :, :, at].reshape(CHIPS, 2, 1, 16, CHUNK)
        pre = jnp.where(act > 0, rows, jnp.zeros_like(rows)).reshape(CHIPS * BLOCK, CHUNK)
        return jnp.dot(query_w[...], pre, preferred_element_type=f32)

    def sib_copy(n):
        return copy_of(
            key_sib_out.at[n], key_sib_in.at[n], sib_send.at[n], sib_recv.at[n], sibling
        )

    def key_copy(n):
        return copy_of(
            key_out.at[n], key_in.at[n], key_send.at[n], key_recv.at[n], dev_z(key_place(n))
        )

    def key_pass_on(n):
        sib_copy(n).wait()
        key_out[n] = (key_own[n] + key_sib_in[n].astype(f32)).astype(bf16)
        key_copy(n).start()

    def key_step(n, carry):
        theirs = key_chunk(1 - core, key_place(n))
        ours = key_chunk(core, key_place(n))
        key_sib_out[n] = theirs.astype(bf16)
        sib_copy(n).start()
        key_own[n] = ours

        @pl.when((n != 0) & (n != 3))
        def _():
            key_pass_on(n - 1)

        return carry

    lax.fori_loop(0, 3, key_step, 0)

    def backward_query(gi):
        acc = jnp.zeros((GROUP * BLOCK, DH), f32)
        for c in range(NCHUNK):
            at = slice(c * CHUNK, (c + 1) * CHUNK)
            act = relu[pl.ds(gi * GROUP, GROUP), :, at].reshape(GROUP, 2, 4, 16, CHUNK)
            rows = grad_rows[pl.ds(gi * GROUP, GROUP), :, :, at].reshape(GROUP, 2, 1, 16, CHUNK)
            pre = jnp.where(act > 0, rows, jnp.zeros_like(rows)).reshape(GROUP * BLOCK, CHUNK)
            acc = acc + jnp.dot(pre, keys[at, :], preferred_element_type=f32)
        return acc.reshape(GROUP, BLOCK, DH)

    def sum_copy(dx, dy):
        i = dx * NY + dy
        return copy_of(
            sum_out.at[chip_at(dx, dy)],
            sum_in.at[i],
            sum_send.at[i],
            sum_recv.at[i],
            dev_chip(dx, dy),
        )

    def backward(n, carry):
        dx = 2 - n + (n // 2) * (3 - 2 * (n % 2))
        g = (x + dx) % NX
        sum_out[pl.ds(g * GROUP, GROUP)] = backward_query(g).astype(bf16)

        def to_chip(dy, c2):
            @pl.when(dx * NY + dy > 0)
            def _():
                sum_copy(dx, dy).start()

            return c2

        lax.fori_loop(0, NY, to_chip, 0)

        @pl.when(n == 0)
        def _():
            key_pass_on(2)

        return carry

    lax.fori_loop(0, NX, backward, 0)
    lax.fori_loop(3, NZ, key_step, 0)

    def wait_sum(i, acc):
        sum_copy(i // NY, i % NY).wait()
        return acc + sum_in[i].astype(f32)

    total_g = lax.fori_loop(1, CHIPS, wait_sum, sum_out[chip].astype(f32))
    total_g = total_g.reshape(2, 8, 8, DH)
    for h in range(NZ):
        back_out[h, 0:8, :] = total_g[0, h]
        back_out[h, 8:16, :] = total_g[1, h]

    def start_back(i, carry):
        copy_of(
            back_out.at[(z + i) % NZ], back_in.at[z], back_send.at[i], back_recv.at[i], dev_z(i)
        ).start()
        return carry

    lax.fori_loop(1, NZ, start_back, 0)
    back_in[pl.ds(z, 1)] = back_out[pl.ds(z, 1)]

    sib_copy(NZ - 1).wait()

    def wait_key(n, acc):
        key_copy(n).wait()
        return acc + key_in[n].astype(f32)

    acc = key_own[NZ - 1] + key_sib_in[NZ - 1].astype(f32)
    key_sum[...] = lax.fori_loop(0, NZ - 1, wait_key, acc).T

    def wait_back(i, carry):
        copy_of(
            back_out.at[(z + i) % NZ],
            back_in.at[(z + NZ - i) % NZ],
            back_send.at[i],
            back_recv.at[i],
            dev_z(i),
        ).wait()
        return carry

    lax.fori_loop(1, NZ, wait_back, 0)
    back[...] = back_in[...].reshape(128, DH)


def finish(back, key_sum, query, weights, query_grad, key_grad, weight_grad):
    head_scale = DH**-0.5
    key_grad[...] = key_sum[...]
    grad = back[...] * head_scale
    spread = jnp.where(iota((16, 128), 0) == iota((16, 128), 1) // 8, 1.0, 0.0)
    w_rows = lax.dot_general(
        spread,
        weights[...].astype(f32),
        (((0,), (1,)), ((), ())),
        preferred_element_type=f32,
    )
    w_rows = jnp.where(iota((128, 8), 0) % 8 == iota((128, 8), 1), w_rows, 0.0)
    query_grad[...] = grad * jnp.sum(w_rows, axis=1, keepdims=True)
    w_grad = jnp.sum(grad * query[...].astype(f32), axis=1, keepdims=True).reshape(16, 8, 1)
    out = jnp.zeros((8, 128), f32)
    for t in range(16):
        out = jnp.where(iota((8, 128), 1) == t, w_grad[t], out)
    weight_grad[...] = out[:, 0:16]


def per_device(query, weights, keys, main_logits, row_weight, offset):
    vmem = pl.BlockSpec(memory_space=pltpu.VMEM)
    anywhere = pl.BlockSpec(memory_space=pl.ANY)
    dma = pltpu.SemaphoreType.DMA
    query = query.reshape(128, DH)
    weights = weights.T
    back, key_sum = pl.pallas_call(
        kernel,
        out_shape=[
            jax.ShapeDtypeStruct((128, DH), f32),
            jax.ShapeDtypeStruct((CHUNK, DH), f32),
        ],
        in_specs=[
            anywhere,
            anywhere,
            anywhere,
            anywhere,
            vmem,
            pl.BlockSpec(memory_space=pltpu.SMEM),
        ],
        out_specs=[vmem, vmem],
        scratch_shapes=[
            pltpu.VMEM((128, DH), bf16),
            pltpu.VMEM((8, 16), bf16),
            pltpu.VMEM((BOTH, DH), bf16),
            pltpu.VMEM((DH, BOTH), bf16),
            pltpu.VMEM((512, KEYS), bf16),
            pltpu.VMEM((2, ROWS, KEYS), bf16),
            pltpu.VMEM((ROWS, KEYS), bf16),
            pltpu.VMEM((NZ, 32, 128), bf16),
            pltpu.VMEM((NZ, 32, 128), bf16),
            pltpu.VMEM((CHIPS, BLOCK + 16, DH), bf16),
            pltpu.VMEM((CHIPS, BLOCK, BOTH), bf16),
            pltpu.VMEM((ROWS, BOTH), f32),
            pltpu.VMEM((ROWS, BOTH), f32),
            pltpu.VMEM((CHIPS, 2, 16, BOTH), bf16),
            pltpu.VMEM((DH, CHIPS * BLOCK), bf16),
            pltpu.VMEM((ROWS, 128), f32),
            pltpu.VMEM((CHIPS, 8, 128), f32),
            pltpu.VMEM((CHIPS, BLOCK, DH), bf16),
            pltpu.VMEM((CHIPS, BLOCK, DH), bf16),
            pltpu.VMEM((NZ, DH, CHUNK), f32),
            pltpu.VMEM((NZ, DH, CHUNK), bf16),
            pltpu.VMEM((NZ, DH, CHUNK), bf16),
            pltpu.VMEM((NZ, DH, CHUNK), bf16),
            pltpu.VMEM((NZ, DH, CHUNK), bf16),
            pltpu.VMEM((NZ, 16, DH), f32),
            pltpu.VMEM((NZ, 16, DH), f32),
            dma((4,)),
            dma((NZ,)),
            dma((NZ,)),
            dma((2,)),
            dma((2,)),
            dma((CHIPS,)),
            dma((CHIPS,)),
            dma((CHIPS,)),
            dma((CHIPS,)),
            dma((CHIPS,)),
            dma((CHIPS,)),
            dma((NZ,)),
            dma((NZ,)),
            dma((NZ,)),
            dma((NZ,)),
            dma((NZ,)),
            dma((NZ,)),
        ],
        compiler_params=pltpu.CompilerParams(
            collective_id=0, has_side_effects=True, vmem_limit_bytes=56 * 2**20
        ),
    )(
        query,
        weights,
        keys,
        main_logits,
        row_weight.reshape(1, 512),
        offset,
    )
    query_grad, key_grad, weight_grad = pl.pallas_call(
        finish,
        out_shape=[
            jax.ShapeDtypeStruct((128, DH), f32),
            jax.ShapeDtypeStruct((CHUNK, DH), f32),
            jax.ShapeDtypeStruct((8, 16), f32),
        ],
        in_specs=[vmem] * 4,
        out_specs=[vmem] * 3,
    )(back, key_sum, query, weights)
    return query_grad.reshape(16, 8, DH), key_grad, weight_grad.T


def solution(mesh):
    in_specs = (P("ctx", "head", None), P("ctx", "head"), P("ctx", None), P(None, "ctx"), P(), P())
    out_specs = (P("ctx", "head", None), P(("ctx", "head"), None), P("ctx", "head"))
    return jax.shard_map(
        per_device, mesh=mesh, in_specs=in_specs, out_specs=out_specs, check_vma=False
    )
```

time: 631 us -> 58.4 us (0.09)
  waiting for transfers between devices: 337 us -> 0 us
  blocking collectives: 174 us -> 0 us
  Pallas kernels: 0 us -> 57 us
  matrix products: 55 us -> 0 us
  local copies, waits for them, and re-layouts: 33.9 us -> 0 us
  other arithmetic: 14.8 us -> 0 us
  between operations: 14.6 us -> 1.29 us
    reduce_scatter x2 -> x0, waiting for transfers between devices: 129 us -> none  [the longest x1 92.7 us: per_device(): lax.psum_scatter(query_acc, 'ctx', scatter_dimension=0, tiled=True)]
    psum x1 -> x0, waiting for transfers between devices: 104 us -> none  [per_device(): scores = lax.psum(partial_scores, 'head')]
    pmax x1 -> x0, blocking collectives: 76.4 us -> none  [global_stats(): peak, tpeak = lax.pmax((peak, tpeak), ('ctx', 'head'))]
    unnamed x6 -> x0, waiting for transfers between devices: 75.1 us -> none
    psum x1 -> x0, blocking collectives: 72.2 us -> none  [global_stats(): lax.psum((exp_total(masked, peak, allowed), exp_total(tmasked, tpeak, all...]
    pallas_call x0 -> x2, Pallas kernels: none -> 57 us  [the longest x1 55.2 us: per_device(): pl.pallas_call(kernel, out_shape=[jax.ShapeDtypeStruct((128, DH), f32), j...]
    dot_general x16 -> x0, matrix products: 55 us -> none  [the longest x4 27.3 us: backward_block(): jnp.einsum('ths,sd->thd', pre_grad, key_block, preferred_element_type=jnp...]
    all_gather x1 -> x0, waiting for transfers between devices: 28.5 us -> none  [per_device(): lax.all_gather(query, 'ctx', axis=0, tiled=True)]
  transfers between devices with their start and end apart: 5 -> 0, of which waited for: 5 -> 0; matrix products, arithmetic and copies ran while one was open for 2% -> 0% of each run, Pallas kernels for 0% -> 0%
where the time goes in v2:
time: 58.4 us; the launch traced here: 58.3 us
  Pallas kernels  57 us (98%)
  between operations  1.29 us (2%)
    pallas_call x1, Pallas kernels, per_device(): pl.pallas_call(kernel, out_shape=[jax.ShapeDtypeStruct((128, DH), f32), j...  55.2 us
    pallas_call x1, Pallas kernels, per_device(): pl.pallas_call(finish, out_shape=[jax.ShapeDtypeStruct((128, DH), f32), j...  1.84 us

profile of v2, /device:TPU:1, one launch (start us, length us, event | category | flops | bytes accessed | tf_op | source)
XLA Modules:
  0.0 58.3 jit_solution(7421870106201033552)
XLA Ops:
  1.3 55.2 %shard_map.85 = (f32[128,128]{1,0:T(8,128)}, f32[256,128]{1,0:T(8,128)}) custom-call(bf16[128,128]{1,0:T(8,128)(2,1)} %bitcast.5, bf16[8,16]{1,0:T(8,128)(2,1)} %bitcast.7, bf16[2048,128]{1,0:T(8,128)(2,1)} %keys_hbm.1, bf16[512,2048]{1,0:T(8,128)(2,1)} %logits_hbm.1, f32[1,512]{1,0:T(1,128)} %bitcast.9, s32[1]{0:T(128)S(6)} %copy.9.offset), custom_call_target="tpu_custom_call" | custom-call | tf_op jit(solution)/shard_map/pallas_call | solution.py:508
  56.5 1.8 %shard_map.86 = (f32[128,128]{1,0:T(8,128)}, f32[256,128]{1,0:T(8,128)}, f32[8,16]{1,0:T(8,128)}) custom-call(f32[128,128]{1,0:T(8,128)} %get-tuple-element.8.back, f32[256,128]{1,0:T(8,128)} %get-tuple-element.9.key_sum, bf16[128,128]{1,0:T(8,128)(2,1)} %bitcast.6, bf16[8,16]{1,0:T(8,128)(2,1)} %bitcast.8), custom_call_target="tpu_custom_call" | custom-call | tf_op jit(solution)/shard_map/pallas_call | solution.py:579

commit v3 on v2

--- a/solution.py
+++ b/solution.py
@@ -22,6 +22,9 @@
 GROUP = 4
 CHUNK = 256
 NCHUNK = BOTH // CHUNK
+LAG = 2
+WHEN = 1
+EARLY = 4
 
 
 def iota(shape, dim):
@@ -75,7 +78,6 @@
     relu,
     score,
     target,
-    grad_rows,
     query_w,
     row_scale,
     stat_in,
@@ -347,11 +349,6 @@
     prob_scale = shares[:, 0:1] * row_scale[:, 0:1]
     target_scale = shares[:, 2:3] * row_scale[:, 0:1]
     score[...] = score[...] * prob_scale - target[...] * target_scale
-    for i in range(NX):
-        for j in range(2):
-            for k in range(GROUP):
-                row = score[i * 8 + j * 4 + k : i * 8 + j * 4 + k + 1, :]
-                grad_rows[i * GROUP + k, j] = jnp.broadcast_to(row, (16, BOTH)).astype(bf16)
 
     def key_place(n):
         return (1 - n % 2) * (4 + n // 2) + (n % 2) * ((7 - n) // 2)
@@ -360,7 +357,17 @@
         first = of_core * KEYS + ((z + dz) % NZ) * CHUNK
         at = pl.ds(pl.multiple_of(first, CHUNK), CHUNK)
         act = relu[:, :, at].reshape(CHIPS, 2, 4, 16, CHUNK)
-        rows = grad_rows[:, :, :, at].reshape(CHIPS, 2, 1, 16, CHUNK)
+        tile = score[:, at]
+        rows = jnp.concatenate(
+            [
+                jnp.broadcast_to(tile[i * 8 + j * 4 + k : i * 8 + j * 4 + k + 1], (16, CHUNK))
+                for i in range(NX)
+                for k in range(GROUP)
+                for j in range(2)
+            ],
+            axis=0,
+        )
+        rows = rows.astype(bf16).reshape(CHIPS, 2, 1, 16, CHUNK)
         pre = jnp.where(act > 0, rows, jnp.zeros_like(rows)).reshape(CHIPS * BLOCK, CHUNK)
         return jnp.dot(query_w[...], pre, preferred_element_type=f32)
 
@@ -386,20 +393,29 @@
         sib_copy(n).start()
         key_own[n] = ours
 
-        @pl.when((n != 0) & (n != 3))
+        @pl.when(n >= EARLY + LAG)
         def _():
-            key_pass_on(n - 1)
-
-        return carry
-
-    lax.fori_loop(0, 3, key_step, 0)
+            key_pass_on(n - LAG)
+
+        return carry
+
+    lax.fori_loop(0, EARLY, key_step, 0)
 
     def backward_query(gi):
         acc = jnp.zeros((GROUP * BLOCK, DH), f32)
         for c in range(NCHUNK):
             at = slice(c * CHUNK, (c + 1) * CHUNK)
             act = relu[pl.ds(gi * GROUP, GROUP), :, at].reshape(GROUP, 2, 4, 16, CHUNK)
-            rows = grad_rows[pl.ds(gi * GROUP, GROUP), :, :, at].reshape(GROUP, 2, 1, 16, CHUNK)
+            tile = score[pl.ds(pl.multiple_of(gi * 8, 8), 8), at]
+            rows = jnp.concatenate(
+                [
+                    jnp.broadcast_to(tile[j * 4 + k : j * 4 + k + 1], (16, CHUNK))
+                    for k in range(GROUP)
+                    for j in range(2)
+                ],
+                axis=0,
+            )
+            rows = rows.astype(bf16).reshape(GROUP, 2, 1, 16, CHUNK)
             pre = jnp.where(act > 0, rows, jnp.zeros_like(rows)).reshape(GROUP * BLOCK, CHUNK)
             acc = acc + jnp.dot(pre, keys[at, :], preferred_element_type=f32)
         return acc.reshape(GROUP, BLOCK, DH)
@@ -428,20 +444,25 @@
 
         lax.fori_loop(0, NY, to_chip, 0)
 
-        @pl.when(n == 0)
+        @pl.when(n == WHEN)
         def _():
-            key_pass_on(2)
+            for k in range(EARLY):
+                key_pass_on(k)
 
         return carry
 
     lax.fori_loop(0, NX, backward, 0)
-    lax.fori_loop(3, NZ, key_step, 0)
-
-    def wait_sum(i, acc):
+    lax.fori_loop(EARLY, NZ, key_step, 0)
+    for k in range(max(NZ - LAG, EARLY), NZ - 1):
+        key_pass_on(k)
+
+    def wait_sum(m, acc):
+        n = m // NY
+        i = (2 - n + (n // 2) * (3 - 2 * (n % 2))) * NY + NY - 1 - m % NY
         sum_copy(i // NY, i % NY).wait()
         return acc + sum_in[i].astype(f32)
 
-    total_g = lax.fori_loop(1, CHIPS, wait_sum, sum_out[chip].astype(f32))
+    total_g = lax.fori_loop(0, CHIPS - 1, wait_sum, sum_out[chip].astype(f32))
     total_g = total_g.reshape(2, 8, 8, DH)
     for h in range(NZ):
         back_out[h, 0:8, :] = total_g[0, h]
@@ -534,7 +555,6 @@
             pltpu.VMEM((CHIPS, BLOCK, BOTH), bf16),
             pltpu.VMEM((ROWS, BOTH), f32),
             pltpu.VMEM((ROWS, BOTH), f32),
-            pltpu.VMEM((CHIPS, 2, 16, BOTH), bf16),
             pltpu.VMEM((DH, CHIPS * BLOCK), bf16),
             pltpu.VMEM((ROWS, 128), f32),
             pltpu.VMEM((CHIPS, 8, 128), f32),

time: 58.4 us -> 56.7 us (0.971)
  Pallas kernels: 57 us -> 55.3 us
    pallas_call x1, Pallas kernels: 55.2 us -> 53.4 us  [per_device(): pl.pallas_call(kernel, out_shape=[jax.ShapeDtypeStruct((128, DH), f32), j...]
where the time goes in v3:
time: 56.7 us; the launch traced here: 56.5 us
  Pallas kernels  55.3 us (98%)
  between operations  1.29 us (2%)
    pallas_call x1, Pallas kernels, per_device(): pl.pallas_call(kernel, out_shape=[jax.ShapeDtypeStruct((128, DH), f32), j...  53.4 us
    pallas_call x1, Pallas kernels, per_device(): pl.pallas_call(finish, out_shape=[jax.ShapeDtypeStruct((128, DH), f32), j...  1.84 us

profile of v3, /device:TPU:1, one launch (start us, length us, event | category | flops | bytes accessed | tf_op | source)
XLA Modules:
  0.0 56.5 jit_solution(6689303824073129375)
XLA Ops:
  1.3 53.4 %shard_map.85 = (f32[128,128]{1,0:T(8,128)}, f32[256,128]{1,0:T(8,128)}) custom-call(bf16[128,128]{1,0:T(8,128)(2,1)} %bitcast.5, bf16[8,16]{1,0:T(8,128)(2,1)} %bitcast.7, bf16[2048,128]{1,0:T(8,128)(2,1)} %keys_hbm.1, bf16[512,2048]{1,0:T(8,128)(2,1)} %logits_hbm.1, f32[1,512]{1,0:T(1,128)} %bitcast.9, s32[1]{0:T(128)S(6)} %copy.9.offset), custom_call_target="tpu_custom_call" | custom-call | tf_op jit(solution)/shard_map/pallas_call | solution.py:529
  54.7 1.8 %shard_map.86 = (f32[128,128]{1,0:T(8,128)}, f32[256,128]{1,0:T(8,128)}, f32[8,16]{1,0:T(8,128)}) custom-call(f32[128,128]{1,0:T(8,128)} %get-tuple-element.8.back, f32[256,128]{1,0:T(8,128)} %get-tuple-element.9.key_sum, bf16[128,128]{1,0:T(8,128)(2,1)} %bitcast.6, bf16[8,16]{1,0:T(8,128)(2,1)} %bitcast.8), custom_call_target="tpu_custom_call" | custom-call | tf_op jit(solution)/shard_map/pallas_call | solution.py:599

commit v4 on v3

--- a/solution.py
+++ b/solution.py
@@ -139,11 +139,15 @@
     load_logits.start()
     barrier = pltpu.get_barrier_semaphore()
 
-    def greet_z(i, carry):
+    def far_first(n):
+        return (1 - n % 2) * (4 + n // 2) + (n % 2) * ((7 - n) // 2)
+
+    def greet_z(n, carry):
+        i = far_first(n)
         pl.semaphore_signal(barrier, inc=1, device_id=dev_z(i), device_id_type=MESH)
         return carry
 
-    lax.fori_loop(1, NZ, greet_z, 0)
+    lax.fori_loop(0, NZ - 1, greet_z, 0)
 
     def greet(i, carry):
         pl.semaphore_signal(
@@ -176,11 +180,11 @@
             send_a.at[(z + i) % NZ], recv_a.at[z], a_send.at[i], a_recv.at[i], dev_z(i)
         )
 
-    def start_a(i, carry):
-        a_copy(i).start()
-        return carry
-
-    lax.fori_loop(1, NZ, start_a, 0)
+    def start_a(n, carry):
+        a_copy(far_first(n)).start()
+        return carry
+
+    lax.fori_loop(0, NZ - 1, start_a, 0)
     recv_a[pl.ds(z, 1)] = send_a[pl.ds(z, 1)]
 
     load_keys.wait()
@@ -251,7 +255,7 @@
     limit = offset[0] - chip * BOTH
 
     def is_allowed():
-        return iota((ROWS, BOTH), 1) <= limit + row_of((ROWS, BOTH), core)
+        return iota((ROWS, BOTH), 1) <= limit + row_of((ROWS, 1), core)
 
     share_logits.wait()
     tlogits = jnp.concatenate([own_logits[0], own_logits[1]], axis=1).astype(f32)
@@ -329,11 +333,11 @@
             stat_in.at[0], stat_in.at[i], st_send.at[i], st_recv.at[i], dev_chip(i // NY, i % NY)
         )
 
-    def start_stat(i, carry):
-        stat_copy(i).start()
-        return carry
-
-    lax.fori_loop(1, CHIPS, start_stat, 0)
+    def start_stat(m, carry):
+        stat_copy((m + 9) % (CHIPS - 1) + 1).start()
+        return carry
+
+    lax.fori_loop(0, CHIPS - 1, start_stat, 0)
 
     def wait_stat(i, carry):
         stat_copy(i).wait()
@@ -349,9 +353,6 @@
     prob_scale = shares[:, 0:1] * row_scale[:, 0:1]
     target_scale = shares[:, 2:3] * row_scale[:, 0:1]
     score[...] = score[...] * prob_scale - target[...] * target_scale
-
-    def key_place(n):
-        return (1 - n % 2) * (4 + n // 2) + (n % 2) * ((7 - n) // 2)
 
     def key_chunk(of_core, dz):
         first = of_core * KEYS + ((z + dz) % NZ) * CHUNK
@@ -378,7 +379,7 @@
 
     def key_copy(n):
         return copy_of(
-            key_out.at[n], key_in.at[n], key_send.at[n], key_recv.at[n], dev_z(key_place(n))
+            key_out.at[n], key_in.at[n], key_send.at[n], key_recv.at[n], dev_z(far_first(n))
         )
 
     def key_pass_on(n):
@@ -387,8 +388,8 @@
         key_copy(n).start()
 
     def key_step(n, carry):
-        theirs = key_chunk(1 - core, key_place(n))
-        ours = key_chunk(core, key_place(n))
+        theirs = key_chunk(1 - core, far_first(n))
+        ours = key_chunk(core, far_first(n))
         key_sib_out[n] = theirs.astype(bf16)
         sib_copy(n).start()
         key_own[n] = ours
@@ -453,8 +454,6 @@
 
     lax.fori_loop(0, NX, backward, 0)
     lax.fori_loop(EARLY, NZ, key_step, 0)
-    for k in range(max(NZ - LAG, EARLY), NZ - 1):
-        key_pass_on(k)
 
     def wait_sum(m, acc):
         n = m // NY
@@ -468,15 +467,18 @@
         back_out[h, 0:8, :] = total_g[0, h]
         back_out[h, 8:16, :] = total_g[1, h]
 
-    def start_back(i, carry):
+    def start_back(n, carry):
+        i = far_first(n)
         copy_of(
             back_out.at[(z + i) % NZ], back_in.at[z], back_send.at[i], back_recv.at[i], dev_z(i)
         ).start()
         return carry
 
-    lax.fori_loop(1, NZ, start_back, 0)
+    lax.fori_loop(0, NZ - 1, start_back, 0)
     back_in[pl.ds(z, 1)] = back_out[pl.ds(z, 1)]
 
+    for k in range(max(NZ - LAG, EARLY), NZ - 1):
+        key_pass_on(k)
     sib_copy(NZ - 1).wait()
 
     def wait_key(n, acc):

time: 56.7 us -> 55.9 us (0.986)
  Pallas kernels: 55.3 us -> 54.5 us
    pallas_call x1, Pallas kernels: 53.4 us -> 52.7 us  [per_device(): pl.pallas_call(kernel, out_shape=[jax.ShapeDtypeStruct((128, DH), f32), j...]
where the time goes in v4:
time: 55.9 us; the launch traced here: 55.8 us
  Pallas kernels  54.5 us (97%)
  between operations  1.29 us (2%)
    pallas_call x1, Pallas kernels, per_device(): pl.pallas_call(kernel, out_shape=[jax.ShapeDtypeStruct((128, DH), f32), j...  52.7 us
    pallas_call x1, Pallas kernels, per_device(): pl.pallas_call(finish, out_shape=[jax.ShapeDtypeStruct((128, DH), f32), j...  1.84 us

profile of v4, /device:TPU:1, one launch (start us, length us, event | category | flops | bytes accessed | tf_op | source)
XLA Modules:
  0.0 55.8 jit_solution(7046187485631437238)
XLA Ops:
  1.3 52.7 %shard_map.85 = (f32[128,128]{1,0:T(8,128)}, f32[256,128]{1,0:T(8,128)}) custom-call(bf16[128,128]{1,0:T(8,128)(2,1)} %bitcast.5, bf16[8,16]{1,0:T(8,128)(2,1)} %bitcast.7, bf16[2048,128]{1,0:T(8,128)(2,1)} %keys_hbm.1, bf16[512,2048]{1,0:T(8,128)(2,1)} %logits_hbm.1, f32[1,512]{1,0:T(1,128)} %bitcast.9, s32[1]{0:T(128)S(6)} %copy.9.offset), custom_call_target="tpu_custom_call" | custom-call | tf_op jit(solution)/shard_map/pallas_call | solution.py:531
  54.0 1.8 %shard_map.86 = (f32[128,128]{1,0:T(8,128)}, f32[256,128]{1,0:T(8,128)}, f32[8,16]{1,0:T(8,128)}) custom-call(f32[128,128]{1,0:T(8,128)} %get-tuple-element.8.back, f32[256,128]{1,0:T(8,128)} %get-tuple-element.9.key_sum, bf16[128,128]{1,0:T(8,128)(2,1)} %bitcast.6, bf16[8,16]{1,0:T(8,128)(2,1)} %bitcast.8), custom_call_target="tpu_custom_call" | custom-call | tf_op jit(solution)/shard_map/pallas_call | solution.py:601

commit v5 on v4

--- a/solution.py
+++ b/solution.py
@@ -387,12 +387,15 @@
         key_out[n] = (key_own[n] + key_sib_in[n].astype(f32)).astype(bf16)
         key_copy(n).start()
 
-    def key_step(n, carry):
+    def key_product(n):
         theirs = key_chunk(1 - core, far_first(n))
         ours = key_chunk(core, far_first(n))
         key_sib_out[n] = theirs.astype(bf16)
         sib_copy(n).start()
         key_own[n] = ours
+
+    def key_step(n, carry):
+        key_product(n)
 
         @pl.when(n >= EARLY + LAG)
         def _():
@@ -453,7 +456,7 @@
         return carry
 
     lax.fori_loop(0, NX, backward, 0)
-    lax.fori_loop(EARLY, NZ, key_step, 0)
+    lax.fori_loop(EARLY, NZ - 1, key_step, 0)
 
     def wait_sum(m, acc):
         n = m // NY
@@ -477,8 +480,9 @@
     lax.fori_loop(0, NZ - 1, start_back, 0)
     back_in[pl.ds(z, 1)] = back_out[pl.ds(z, 1)]
 
-    for k in range(max(NZ - LAG, EARLY), NZ - 1):
+    for k in range(max(NZ - 1 - LAG, EARLY), NZ - 1):
         key_pass_on(k)
+    key_product(NZ - 1)
     sib_copy(NZ - 1).wait()
 
     def wait_key(n, acc):

time: 55.9 us -> 55.9 us (level)
  no operation moved by 1% of the time
where the time goes in v5:
time: 55.9 us; the launch traced here: 55.8 us
  Pallas kernels  54.5 us (97%)
  between operations  1.29 us (2%)
    pallas_call x1, Pallas kernels, per_device(): pl.pallas_call(kernel, out_shape=[jax.ShapeDtypeStruct((128, DH), f32), j...  52.7 us
    pallas_call x1, Pallas kernels, per_device(): pl.pallas_call(finish, out_shape=[jax.ShapeDtypeStruct((128, DH), f32), j...  1.84 us

profile of v5, /device:TPU:1, one launch (start us, length us, event | category | flops | bytes accessed | tf_op | source)
XLA Modules:
  0.0 55.8 jit_solution(17956289081021564909)
XLA Ops:
  1.3 52.7 %shard_map.85 = (f32[128,128]{1,0:T(8,128)}, f32[256,128]{1,0:T(8,128)}) custom-call(bf16[128,128]{1,0:T(8,128)(2,1)} %bitcast.5, bf16[8,16]{1,0:T(8,128)(2,1)} %bitcast.7, bf16[2048,128]{1,0:T(8,128)(2,1)} %keys_hbm.1, bf16[512,2048]{1,0:T(8,128)(2,1)} %logits_hbm.1, f32[1,512]{1,0:T(1,128)} %bitcast.9, s32[1]{0:T(128)S(6)} %copy.9.offset), custom_call_target="tpu_custom_call" | custom-call | tf_op jit(solution)/shard_map/pallas_call | solution.py:535
  54.0 1.8 %shard_map.86 = (f32[128,128]{1,0:T(8,128)}, f32[256,128]{1,0:T(8,128)}, f32[8,16]{1,0:T(8,128)}) custom-call(f32[128,128]{1,0:T(8,128)} %get-tuple-element.8.back, f32[256,128]{1,0:T(8,128)} %get-tuple-element.9.key_sum, bf16[128,128]{1,0:T(8,128)(2,1)} %bitcast.6, bf16[8,16]{1,0:T(8,128)(2,1)} %bitcast.8), custom_call_target="tpu_custom_call" | custom-call | tf_op jit(solution)/shard_map/pallas_call | solution.py:605
